TPU v7x, 32 devices: a whole 2x2x4 slice. The times are simulated.
32 devices in a mesh: member: 2 (over y), face: 4 (over z), slot: 2 (over x), chan: 2 (over core).
Axes of the slice: x: 2, y: 2, z: 4, core: 2. Of those that a mesh axis runs over, the one named last changes fastest.
Arguments:
- observed: bfloat16 [16384, 128], P(('member', 'face', 'slot')), parts along dimension 0, may hold values from -6 to 6
- target_face: int32 [16384, 1], P(('member', 'face', 'slot')), parts along dimension 0, may hold values from 0 to 3; in each aligned block of 1024 rows (0 to 1023, 1024 to 2047, ...) at most 512 rows name the same one
- target_cell: int32 [16384], P(('member', 'face', 'slot')), parts along dimension 0, may hold values from 0 to 319
- node_embed: bfloat16 [1280, 1024], P(('face', 'slot'), 'chan'), may hold values from -6 to 6
- neighbours: int32 [6, 1280], P(None, ('face', 'slot')), may hold values from 0 to 223, as said below
- edge_weight: float32 [6, 1280], P(None, ('face', 'slot')), may hold values from 0.05 to 0.35
- w_embed: bfloat16 [128, 1024], replicated, may hold values from -0.5 to 0.5
- w_key: bfloat16 [1024, 1024], P(None, 'chan'), may hold values from -0.1875 to 0.1875
- w_mix: bfloat16 [1024, 1024], P(None, 'chan'), may hold values from -0.1875 to 0.1875
- w_back: bfloat16 [1024, 1024], P('chan'), may hold values from -0.1875 to 0.1875
- w_out: bfloat16 [1024, 128], P('chan'), may hold values from -0.1875 to 0.1875
Outputs:
- predicted: bfloat16 [16384, 128], P(('member', 'face', 'slot')), parts along dimension 0
- state: bfloat16 [2560, 1024], P(('member', 'face', 'slot'), 'chan'), parts along dimension 0
There are 2 independent parts, one for each index of `member`. A program takes and returns all parts, laid end to end along the dimension named above; an argument that names none is the same for every part. Nothing has to cross between parts.
Inputs may be any that keep to these rules, and one draw needn't show every extreme that they name: `target_face`: within the rows of one device (1024) no face region is named by more than 512 rows, and in some device one face region is named by exactly 512 rows. `neighbours`: entry [j, n] lies within 32 positions of n's own position, which is (n mod 160) + 32.
All inputs are finite; a program needn't handle non-finite values.
Results may differ from a plain program's by a relative error of at most 0.014.
Values may be sent and summed in bfloat16 or wider, within the bound.
A program may use at most 64 MiB of HBM per device.

v0:
```python
import math

import jax
import jax.numpy as jnp
from jax import lax
from jax.sharding import PartitionSpec as P

HD = 64
HALO = 32


def with_halo(cells, sides, width):
    for axis, dim in sides:
        count = lax.axis_size(axis)
        head = lax.slice_in_dim(cells, 0, width, axis=dim)
        tail = lax.slice_in_dim(cells, cells.shape[dim] - width, cells.shape[dim], axis=dim)
        cells = jnp.concatenate(
            [
                lax.ppermute(tail, axis, [(i, (i + 1) % count) for i in range(count)]),
                cells,
                lax.ppermute(head, axis, [((i + 1) % count, i) for i in range(count)]),
            ],
            axis=dim,
        )
    return cells


def body(
    observed,
    target_face,
    target_cell,
    node_embed,
    neighbours,
    edge_weight,
    w_embed,
    w_key,
    w_mix,
    w_back,
    w_out,
):
    faces = lax.axis_size("face")
    row_count = observed.shape[0]
    capacity = 2 * row_count // faces
    local_width = w_key.shape[1]
    local_heads = local_width // HD
    channel_start = lax.axis_index("chan") * local_width
    face_of = target_face[:, 0]
    member_of = (face_of[:, None] == jnp.arange(faces, dtype=jnp.int32)[None, :]).astype(jnp.int32)
    position = jnp.sum((jnp.cumsum(member_of, axis=0) - 1) * member_of, axis=1)
    slot_index = face_of * capacity + position
    cell_buffer = jnp.full((faces * capacity,), -1, jnp.int32).at[slot_index].set(target_cell)
    embedded = jax.nn.gelu(jnp.dot(observed, w_embed, preferred_element_type=jnp.float32)).astype(
        jnp.bfloat16
    )
    keys = jnp.dot(embedded, w_key, preferred_element_type=jnp.float32).astype(jnp.bfloat16)
    values = lax.dynamic_slice_in_dim(embedded, channel_start, local_width, 1)
    keys, values = (keys, values)
    key_buffer = jnp.zeros((faces * capacity, local_width), jnp.bfloat16).at[slot_index].set(keys)
    value_buffer = (
        jnp.zeros((faces * capacity, local_width), jnp.bfloat16).at[slot_index].set(values)
    )
    keys_in, values_in, cells_in = (
        lax.all_to_all(key_buffer, "face", split_axis=0, concat_axis=0, tiled=True),
        lax.all_to_all(value_buffer, "face", split_axis=0, concat_axis=0, tiled=True),
        lax.all_to_all(cell_buffer, "face", split_axis=0, concat_axis=0, tiled=True),
    )
    valid = cells_in >= 0
    safe_cell = jnp.maximum(cells_in, 0)
    queries = lax.all_gather(node_embed, "slot", axis=0, tiled=True)
    face_nodes = queries.shape[0]
    received = keys_in.shape[0]
    picked = queries[safe_cell]
    score = jnp.einsum(
        "rhd,rhd->rh",
        picked.reshape(received, local_heads, HD),
        keys_in.reshape(received, local_heads, HD),
        preferred_element_type=jnp.float32,
    ) / math.sqrt(HD)
    attend = jnp.where(valid[:, None], jax.nn.sigmoid(score), 0.0)
    contrib = jnp.repeat(attend, HD, axis=1) * values_in.astype(jnp.float32)
    node_range = jnp.arange(face_nodes, dtype=jnp.int32)
    onehot = ((safe_cell[:, None] == node_range[None, :]) & valid[:, None]).astype(jnp.float32)
    numer = jnp.einsum(
        "rn,rc->nc",
        onehot,
        contrib,
        precision=lax.Precision.HIGHEST,
        preferred_element_type=jnp.float32,
    )
    denom = jnp.einsum(
        "rn,rh->nh",
        onehot,
        attend,
        precision=lax.Precision.HIGHEST,
        preferred_element_type=jnp.float32,
    )
    numer, denom = (
        lax.psum_scatter(
            numer.astype(jnp.bfloat16), "slot", scatter_dimension=0, tiled=True
        ).astype(jnp.float32),
        lax.psum_scatter(
            denom.astype(jnp.bfloat16), "slot", scatter_dimension=0, tiled=True
        ).astype(jnp.float32),
    )
    latent = (
        node_embed.astype(jnp.float32) + numer / (1.0 + jnp.repeat(denom, HD, axis=1))
    ).astype(jnp.bfloat16)
    widened = with_halo(latent, ((("face", "slot"), 0),), HALO)
    summed = jnp.sum(
        edge_weight[:, :, None] * widened[neighbours].astype(jnp.float32), axis=0
    ).astype(jnp.bfloat16)
    mixed = jnp.dot(
        lax.all_gather(summed, "chan", axis=1, tiled=True),
        w_mix,
        preferred_element_type=jnp.float32,
    )
    hidden = jax.nn.gelu(mixed).astype(jnp.bfloat16)
    update = lax.psum_scatter(
        jnp.dot(hidden, w_back, preferred_element_type=jnp.float32).astype(jnp.bfloat16),
        "chan",
        scatter_dimension=1,
        tiled=True,
    ).astype(jnp.float32)
    state = (latent.astype(jnp.float32) + update).astype(jnp.bfloat16)
    face_state = lax.all_gather(state, "slot", axis=0, tiled=True)
    row_terms = jnp.dot(face_state[safe_cell], w_out, preferred_element_type=jnp.float32)
    answers = lax.psum(row_terms.astype(jnp.bfloat16), "chan")
    returned = lax.all_to_all(answers, "face", split_axis=0, concat_axis=0, tiled=True)
    predicted = returned[slot_index]
    return (predicted, state)


def solution(mesh):
    in_specs = (
        P(("member", "face", "slot"), None),
        P(("member", "face", "slot"), None),
        P(("member", "face", "slot")),
        P(("face", "slot"), "chan"),
        P(None, ("face", "slot")),
        P(None, ("face", "slot")),
        P(),
        P(None, "chan"),
        P(None, "chan"),
        P("chan", None),
        P("chan", None),
    )
    out_specs = (P(("member", "face", "slot"), None), P(("member", "face", "slot"), "chan"))
    return jax.shard_map(body, mesh=mesh, in_specs=in_specs, out_specs=out_specs, check_vma=False)
```

profile of v0, /device:TPU:0, one launch (start us, length us, event | category | flops | bytes accessed | tf_op | source)
XLA Modules:
  0.0 277.1 jit_solution(8348656541998855606)
XLA Ops:
  7.2 0.8 fusion.46
  8.0 1.1 reduce-window.6
  9.1 0.2 slice_reduce_fusion
  9.3 0.2 reduce-window.9
  9.5 0.1 add_bitcast_fusion
  9.6 0.7 fusion.45
  10.3 0.7 compare_select_fusion
  11.0 5.0 %scatter_custom_fusion = s32[2048]{0:T(1024)} fusion(s32[1024]{0:T(1024)S(1)} %bitcast.61, s32[1024]{0:T(1024)} %param.13, s32[]{:T(128)} %constant.14.clone.1), kind=kCustom, calls=%fused_computation.73 | custom fusion | bytes 8704 | tf_op jit(solution)/shard_map/scatter | solution.py:51
  16.0 6.3 %all-to-all-start = ((s32[4,512,1]{1,2,0:T(1,128)}), s32[4,512,1]{1,2,0:T(1,128)S(1)}, u32[]{:S(2)}, u32[]{:S(2)}) async-start(s32[4,512,1]{1,2,0:T(1,128)} %bitcast.5), calls=%async_computation | async-start | bytes 16384 | tf_op jit(solution)/shard_map/all_to_all | solution.py:65
  22.3 2.5 fusion.7
  24.8 1.3 copy-done.6
  26.1 2.2 convolution_convert_fusion.1
  28.4 6.3 %scatter_custom_fusion.1 = bf16[2048,512]{1,0:T(8,128)(2,1)S(1)} fusion(s32[1024]{0:T(1024)S(1)} %bitcast.62, bf16[1024,512]{1,0:T(8,128)(2,1)} %convolution_convert_fusion.1, bf16[]{:T(256)} %constant.19.clone.1), kind=kCustom, calls=%fused_computation.39 | custom fusion | bytes 2097664 | tf_op jit(solution)/shard_map/scatter | solution.py:58
  34.6 2.4 copy.22
  37.0 5.1 %all-to-all-start.1 = ((bf16[4,512,512]{1,2,0:T(8,128)(2,1)}), bf16[4,512,512]{1,2,0:T(8,128)(2,1)S(1)}, u32[]{:S(2)}, u32[]{:S(2)}) async-start(bf16[4,512,512]{1,2,0:T(8,128)(2,1)} %copy.22), calls=%async_computation.1 | async-start | bytes 4194304 | tf_op jit(solution)/shard_map/all_to_all | solution.py:63
  42.1 7.2 %scatter_custom_fusion.2 = bf16[2048,512]{1,0:T(8,128)(2,1)} fusion(s32[1024]{0:T(1024)S(1)} %bitcast.63, bf16[1024,1024]{1,0:T(8,128)(2,1)} %copy-done.6, s32[]{:T(128)} %constant.16.clone.1, s32[]{:T(128)S(6)} %select_n.21, bf16[]{:T(256)} %constant.19.clone.1), kind=kCustom, calls=%fused_computation.36 | custom fusion | bytes 3146756 | tf_op jit(solution)/shard_map/scatter | solution.py:60
  49.3 40.5 %all-to-all-done.1 = bf16[4,512,512]{1,2,0:T(8,128)(2,1)S(1)} async-done(((bf16[4,512,512]{1,2,0:T(8,128)(2,1)}), bf16[4,512,512]{1,2,0:T(8,128)(2,1)S(1)}, u32[]{:S(2)}, u32[]{:S(2)}) %all-to-all-start.1) | async-done | bytes 2097184 | tf_op jit(solution)/shard_map/all_to_all | solution.py:63
  89.8 1.3 copy-done.2
  91.1 3.6 %all-to-all-start.2 = ((bf16[4,512,512]{2,1,0:T(8,128)(2,1)}), bf16[4,512,512]{2,1,0:T(8,128)(2,1)S(1)}, u32[]{:S(2)}, u32[]{:S(2)}) async-start(bf16[4,512,512]{2,1,0:T(8,128)(2,1)} %bitcast.52), calls=%async_computation.2 | async-start | bytes 4194304 | tf_op jit(solution)/shard_map/all_to_all | solution.py:64
  94.7 0.0 reduce-scatter.10.cloned.1.call-start
  94.7 6.4 %all_gather.9 = bf16[320,512]{1,0:T(8,128)(2,1)S(1)} all-gather(bf16[160,512]{1,0:T(8,128)(2,1)} %param.14), channel_id=1, replica_groups=mesh['member'=2,'face'=4,'slot'=2,'chan'=2] {'slot'}, dimensions={0}, use_global_device_ids=true | all-gather | bytes 491520 | tf_op jit(solution)/shard_map/all_gather | solution.py:69
  101.2 9.2 %gather_fusion = bf16[2048,512]{1,0:T(8,128)(2,1)} fusion(bf16[320,512]{1,0:T(8,128)(2,1)S(1)} %all_gather.9, s32[2048]{0:T(1024)S(1)} %broadcast_clamp_fusion), kind=kCustom, calls=%fused_computation | custom fusion | bytes 4202496 | tf_op jit(solution)/shard_map/gather | solution.py:72
  110.3 4.0 %copy.34 = bf16[2048,512]{0,1:T(8,128)(2,1)} copy(bf16[2048,512]{1,0:T(8,128)(2,1)} %gather_fusion) | data formatting | bytes 4194304 | tf_op jit(solution)/shard_map/reshape | solution.py:75
  114.4 4.5 %copy.23 = bf16[4,512,512]{1,0,2:T(4,128)(2,1)} copy(bf16[4,512,512]{1,2,0:T(8,128)(2,1)} %copy-done.2) | data formatting | bytes 4194304 | tf_op jit(solution)/shard_map/all_to_all | solution.py:63
  118.9 4.5 %reshape.72 = bf16[2048,8,64]{0,2,1:T(8,128)(2,1)} reshape(bf16[4,512,512]{1,0,2:T(4,128)(2,1)} %copy.23) | data formatting | bytes 4194304 | tf_op jit(solution)/shard_map/reshape | solution.py:76
  123.4 19.0 %all-to-all-done.2 = bf16[4,512,512]{2,1,0:T(8,128)(2,1)S(1)} async-done(((bf16[4,512,512]{2,1,0:T(8,128)(2,1)}), bf16[4,512,512]{2,1,0:T(8,128)(2,1)S(1)}, u32[]{:S(2)}, u32[]{:S(2)}) %all-to-all-start.2) | async-done | bytes 2097184 | tf_op jit(solution)/shard_map/all_to_all | solution.py:64
  142.3 2.7 bitcast_convert_fusion
  145.0 5.5 %copy.31 = f32[2048,512]{0,1:T(8,128)} copy(f32[2048,512]{1,0:T(8,128)} %bitcast_convert_fusion) | data formatting | bytes 8388608 | tf_op jit(solution)/shard_map/convert_element_type | solution.py:80
  150.6 2.5 fusion.8
  153.1 1.3 fusion.23
  154.4 2.3 bitcast_multiply_fusion
  156.7 0.8 copy.32
  157.5 0.0 reduce-scatter.10.cloned.1.call-update
  157.5 0.0 reduce-scatter.6.cloned.1.call-start
  157.6 6.6 %fusion.20 = bf16[320,512]{1,0:T(8,128)(2,1)} fusion(f32[2048,512]{0,1:T(8,128)} %bitcast_multiply_fusion, s32[2048]{0:T(1024)S(1)} %bitcast.60, pred[2048]{0:T(1024)(128)(4,1)S(1)} %bitcast.68), kind=kOutput, calls=%fused_computation.33 | convolution fusion | flops 4028661760 | bytes 4532224 | tf_op jit(solution)/shard_map/rn,rc->nc/dot_general | solution.py:83
  164.2 0.0 reduce-scatter.6.cloned.1.call-update
  164.2 0.0 reduce-scatter.8.cloned.1.call-start
  164.3 0.1 reshape.85
  164.4 2.3 reduce-scatter.10.cloned.1.call-done
  166.7 0.8 copy.33
  167.5 0.1 copy.25
  167.6 0.2 broadcast_in_dim.40
  167.9 0.2 add.72
  168.1 13.3 %reduce-scatter.6.cloned.1.call-done = bf16[160,512]{1,0:T(8,128)(2,1)} async-done(((bf16[320,512]{1,0:T(8,128)(2,1)}), bf16[160,512]{1,0:T(8,128)(2,1)}) %reduce-scatter.6.cloned.1.call-update) | async-done | bytes 163856 | tf_op jit(solution)/shard_map/reduce_scatter | solution.py:98
  181.3 1.0 add_convert_fusion.1
  182.3 0.4 collective-permute-start
  182.7 4.4 %collective-permute-start.1 = (bf16[32,512]{1,0:T(8,128)(2,1)S(1)}, bf16[32,512]{1,0:T(8,128)(2,1)S(1)}, u32[]{:S(2)}, u32[]{:S(2)}) collective-permute-start(bf16[32,512]{1,0:T(8,128)(2,1)S(1)} %get-tuple-element.3), channel_id=1, source_target_pairs={{2,0},{4,2},{6,4},{8,6},{10,8},{12,10},{14,12},{0,14},{3,1},{5,3},... | collective-permute-start | bytes 98312 | tf_op jit(solution)/shard_map/ppermute | solution.py:21
  187.1 1.9 collective-permute-done
  189.0 4.1 %gather_fusion.1 = bf16[960,512]{1,0:T(8,128)(2,1)S(1)} fusion(bf16[224,512]{1,0:T(8,128)(2,1)S(1)} %pad_maximum_fusion, s32[1024]{0:T(1024)S(1)} %pad_clamp_fusion), kind=kCustom, calls=%fused_computation.1 | custom fusion | bytes 1969920 | tf_op jit(solution)/shard_map/gather | solution.py:110
  193.1 0.3 fusion.13
  193.4 2.0 all_gather.10
  195.4 2.9 %convolution_convert_fusion.2 = bf16[160,1024]{1,0:T(8,128)(2,1)} fusion(bf16[512,1024]{1,0:T(8,128)(2,1)} %param.20, bf16[160,1024]{1,0:T(8,128)(2,1)S(1)} %all_gather.10, bf16[1024,512]{1,0:T(8,128)(2,1)} %param.19), kind=kOutput, calls=%fused_computation.34 | convolution fusion | flops 336445440 | bytes 2752512 | tf_op jit(solution)/shard_map/dot_general | solution.py:119
  198.4 0.0 all-reduce.2.cloned.1.call-start
  198.4 9.2 %reduce-scatter.8.cloned.1.call-done = bf16[160,512]{1,0:T(8,128)(2,1)} async-done(((bf16[160,1024]{1,0:T(8,128)(2,1)}), bf16[160,512]{1,0:T(8,128)(2,1)}) %reduce-scatter.8.cloned.1.call-update) | async-done | bytes 163856 | tf_op jit(solution)/shard_map/reduce_scatter | solution.py:118
  207.7 1.0 add_convert_fusion
  208.6 0.7 copy-done.5
  209.3 7.0 %all_gather.11 = bf16[320,512]{1,0:T(8,128)(2,1)S(1)} all-gather(bf16[160,512]{1,0:T(8,128)(2,1)S(1)} %add_convert_fusion), channel_id=1, replica_groups=mesh['member'=2,'face'=4,'slot'=2,'chan'=2] {'slot'}, dimensions={0}, use_global_device_ids=true | all-gather | bytes 491520 | tf_op jit(solution)/shard_map/all_gather | solution.py:125
  216.3 7.5 %gather_fusion.2 = bf16[2048,512]{1,0:T(8,128)(2,1)S(1)} fusion(bf16[320,512]{1,0:T(8,128)(2,1)S(1)} %all_gather.11, s32[2048]{0:T(1024)S(1)} %broadcast_clamp_fusion), kind=kCustom, calls=%fused_computation.2 | custom fusion | bytes 4202496 | tf_op jit(solution)/shard_map/gather | solution.py:126
  223.9 2.4 convolution_convert_fusion
  226.3 0.0 all-reduce.2.cloned.1.call-update
  226.3 20.1 %all-reduce.2.cloned.1.call-done = bf16[4,512,128]{2,1,0:T(8,128)(2,1)} async-done(((bf16[4,512,128]{2,1,0:T(8,128)(2,1)}), bf16[4,512,128]{2,1,0:T(8,128)(2,1)}) %all-reduce.2.cloned.1.call-update) | async-done | bytes 524304 | tf_op jit(solution)/shard_map/psum | solution.py:127
  246.4 4.9 %all-to-all-start.3 = ((bf16[4,512,128]{2,1,0:T(8,128)(2,1)}), bf16[4,512,128]{2,1,0:T(8,128)(2,1)S(1)}, u32[]{:S(2)}, u32[]{:S(2)}) async-start(bf16[4,512,128]{2,1,0:T(8,128)(2,1)} %all-reduce.2.cloned.1.call-done), calls=%async_computation.5 | async-start | bytes 1048576 | tf_op jit(solution)/shard_map/all_to_all | solution.py:128
  251.3 14.9 %all-to-all-done.3 = bf16[4,512,128]{2,1,0:T(8,128)(2,1)S(1)} async-done(((bf16[4,512,128]{2,1,0:T(8,128)(2,1)}), bf16[4,512,128]{2,1,0:T(8,128)(2,1)S(1)}, u32[]{:S(2)}, u32[]{:S(2)}) %all-to-all-start.3) | async-done | bytes 524320 | tf_op jit(solution)/shard_map/all_to_all | solution.py:128
  266.2 4.3 %gather_fusion.3 = bf16[1024,128]{1,0:T(8,128)(2,1)} fusion(bf16[2048,128]{1,0:T(8,128)(2,1)S(1)} %bitcast.51, s32[1024]{0:T(1024)S(1)} %broadcast_clamp_fusion.1), kind=kCustom, calls=%fused_computation.3 | custom fusion | bytes 528384 | tf_op jit(solution)/shard_map/gather | solution.py:129
  (29 shorter events, 0.2 us)
Async XLA Ops:
  7.2 19.0 %copy-start = (bf16[1024,512]{1,0:T(8,128)(2,1)S(1)}, bf16[1024,512]{1,0:T(8,128)(2,1)}, u32[]{:S(2)}) copy-start(bf16[1024,512]{1,0:T(8,128)(2,1)} %param.18) | copy-start | bytes 3145732
  16.0 21.0 %all-to-all-start = ((s32[4,512,1]{1,2,0:T(1,128)}), s32[4,512,1]{1,2,0:T(1,128)S(1)}, u32[]{:S(2)}, u32[]{:S(2)}) async-start(s32[4,512,1]{1,2,0:T(1,128)} %bitcast.5), calls=%async_computation | async-start | bytes 16384 | tf_op jit(solution)/shard_map/all_to_all | solution.py:65
  24.8 1.3 copy-start.6
  37.0 52.7 %all-to-all-start.1 = ((bf16[4,512,512]{1,2,0:T(8,128)(2,1)}), bf16[4,512,512]{1,2,0:T(8,128)(2,1)S(1)}, u32[]{:S(2)}, u32[]{:S(2)}) async-start(bf16[4,512,512]{1,2,0:T(8,128)(2,1)} %copy.22), calls=%async_computation.1 | async-start | bytes 4194304 | tf_op jit(solution)/shard_map/all_to_all | solution.py:63
  89.8 1.3 copy-start.2
  91.1 51.3 %all-to-all-start.2 = ((bf16[4,512,512]{2,1,0:T(8,128)(2,1)}), bf16[4,512,512]{2,1,0:T(8,128)(2,1)S(1)}, u32[]{:S(2)}, u32[]{:S(2)}) async-start(bf16[4,512,512]{2,1,0:T(8,128)(2,1)} %bitcast.52), calls=%async_computation.2 | async-start | bytes 4194304 | tf_op jit(solution)/shard_map/all_to_all | solution.py:64
  94.7 72.0 %reduce-scatter.10.cloned.1.call-start = ((), (), s32[]{:S(2)}) async-start(), calls=%async_computation.10 | async-start | bytes 122880
  145.0 5.5 %copy-start.3 = (bf16[2048,512]{0,1:T(8,128)(2,1)S(1)}, bf16[2048,512]{0,1:T(8,128)(2,1)}, u32[]{:S(2)}) copy-start(bf16[2048,512]{0,1:T(8,128)(2,1)} %copy.34) | copy-start | bytes 6291460
  150.6 3.8 %copy-start.1 = (f32[2048,512]{0,1:T(8,128)S(1)}, f32[2048,512]{0,1:T(8,128)}, u32[]{:S(2)}) copy-start(f32[2048,512]{0,1:T(8,128)} %copy.31) | copy-start | bytes 12582916
  157.5 6.8 %copy-start.8 = (s32[6,160]{1,0:T(8,128)S(1)}, s32[6,160]{1,0:T(8,128)}, u32[]{:S(2)}) copy-start(s32[6,160]{1,0:T(8,128)} %param.15) | copy-start | bytes 11524
  157.5 23.8 %reduce-scatter.6.cloned.1.call-start = ((), (), s32[]{:S(2)}) async-start(), calls=%async_computation.7 | async-start | bytes 491520 | tf_op jit(solution)/shard_map/reduce_scatter | solution.py:98
  164.2 17.1 %copy-start.4 = (bf16[160,512]{1,0:T(8,128)(2,1)S(1)}, bf16[160,512]{1,0:T(8,128)(2,1)}, u32[]{:S(2)}) copy-start(bf16[160,512]{1,0:T(8,128)(2,1)} %param.14) | copy-start | bytes 491524
  164.2 43.5 %reduce-scatter.8.cloned.1.call-start = ((), (), s32[]{:S(2)}) async-start(), calls=%async_computation.8 | async-start | bytes 491520 | tf_op jit(solution)/shard_map/reduce_scatter | solution.py:118
  182.3 6.7 %collective-permute-start = (bf16[32,512]{1,0:T(8,128)(2,1)S(1)}, bf16[32,512]{1,0:T(8,128)(2,1)S(1)}, u32[]{:S(2)}, u32[]{:S(2)}) collective-permute-start(bf16[32,512]{1,0:T(8,128)(2,1)S(1)} %get-tuple-element.2), channel_id=1, source_target_pairs={{0,2},{2,4},{4,6},{6,8},{8,10},{10,12},{12,14},{14,0},{1,3},{3,5},... | collective-permute-start | bytes 98312 | tf_op jit(solution)/shard_map/ppermute | solution.py:19
  182.7 6.3 %collective-permute-start.1 = (bf16[32,512]{1,0:T(8,128)(2,1)S(1)}, bf16[32,512]{1,0:T(8,128)(2,1)S(1)}, u32[]{:S(2)}, u32[]{:S(2)}) collective-permute-start(bf16[32,512]{1,0:T(8,128)(2,1)S(1)} %get-tuple-element.3), channel_id=1, source_target_pairs={{2,0},{4,2},{6,4},{8,6},{10,8},{12,10},{14,12},{0,14},{3,1},{5,3},... | collective-permute-start | bytes 98312 | tf_op jit(solution)/shard_map/ppermute | solution.py:21
  189.0 4.1 %copy-start.7 = (f32[6,160]{1,0:T(8,128)S(1)}, f32[6,160]{1,0:T(8,128)}, u32[]{:S(2)}) copy-start(f32[6,160]{1,0:T(8,128)} %param.16) | copy-start | bytes 11524
  198.4 48.0 %all-reduce.2.cloned.1.call-start = ((), (), s32[]{:S(2)}) async-start(), calls=%async_computation.9 | async-start | bytes 1048576 | tf_op jit(solution)/shard_map/psum | solution.py:127
  208.6 0.7 copy-start.5
  246.4 19.8 %all-to-all-start.3 = ((bf16[4,512,128]{2,1,0:T(8,128)(2,1)}), bf16[4,512,128]{2,1,0:T(8,128)(2,1)S(1)}, u32[]{:S(2)}, u32[]{:S(2)}) async-start(bf16[4,512,128]{2,1,0:T(8,128)(2,1)} %all-reduce.2.cloned.1.call-done), calls=%async_computation.5 | async-start | bytes 1048576 | tf_op jit(solution)/shard_map/all_to_all | solution.py:128
Sparse Core Ops, SparseCore 0:
  157.6 9.0 reduce-scatter.9
  168.9 12.3 reduce-scatter.5
  198.5 9.1 reduce-scatter.7
  226.4 19.9 all-reduce.1
where the time goes:
time: 278 us; the launch traced here: 277 us
  waiting for transfers between devices  121 us (44%)
  local copies, waits for them, and re-layouts  70.2 us (25%)
  starting transfers between devices  24.8 us (9%)
  matrix products  18 us (6%)
  blocking collectives  15.5 us (6%)
  between operations  14 us (5%)
  other arithmetic  13.4 us (5%)
    all_to_all x1, waiting for transfers between devices, body(): lax.all_to_all(key_buffer, 'face', split_axis=0, concat_axis=0, tiled=True)  40.5 us
    psum x1, waiting for transfers between devices, body(): answers = lax.psum(row_terms.astype(jnp.bfloat16), 'chan')  20.1 us
    all_to_all x1, waiting for transfers between devices, body(): lax.all_to_all(value_buffer, 'face', split_axis=0, concat_axis=0, tiled=T...  19 us
    all_to_all x1, waiting for transfers between devices, body(): lax.all_to_all(answers, 'face', split_axis=0, concat_axis=0, tiled=True)  14.9 us
    scatter x2, local copies, waits for them, and re-layouts, body(): jnp.zeros((faces * capacity, local_width), jnp.bfloat16).at[slot_index]  13.4 us
    reduce_scatter x1, waiting for transfers between devices, body(): lax.psum_scatter(numer.astype(jnp.bfloat16), 'slot', scatter_dimension=0,...  13.3 us
    reduce_scatter x1, waiting for transfers between devices, body(): lax.psum_scatter(jnp.dot(hidden, w_back, preferred_element_type=jnp.float...  9.24 us
    gather x1, local copies, waits for them, and re-layouts, body(): picked = queries[safe_cell]  9.18 us
  transfers between devices with their start and end apart: 10, of which 8 were waited for; matrix products, arithmetic and copies ran while one was open for 18% of the time, Pallas kernels for 0%

commit v1 on v0

v1 whole, which is shorter than its diff:
```python
import functools

import jax
import jax.numpy as jnp
from jax import lax
from jax.experimental import pallas as pl
from jax.experimental.pallas import tpu as pltpu
from jax.sharding import PartitionSpec as P

HD = 64
HALO = 32
LANES = 128
MESH = pl.DeviceIdType.MESH
F32 = jnp.float32
BF16 = jnp.bfloat16


def dot(a, b):
    return jnp.dot(a, b, preferred_element_type=F32)


def dot_tn(a, b):
    return lax.dot_general(a, b, (((0,), (0,)), ((), ())), preferred_element_type=F32)


def dot_nt(a, b):
    return lax.dot_general(a, b, (((1,), (1,)), ((), ())), preferred_element_type=F32)


def ones_where(mask):
    return jnp.where(mask, 1.0, 0.0).astype(BF16)


def two_parts(x):
    high = x.astype(BF16)
    return high, (x - high.astype(F32)).astype(BF16)


def kernel(
    faces,
    slots,
    observed,
    face_row,
    cell_row,
    node_col,
    node_embed,
    neighbours,
    edge_weight,
    w_embed,
    w_key,
    w_mix,
    w_back,
    w_out,
    predicted,
    state_out,
    rows_out,
    rows_in,
    cells_out,
    cells_in,
    queries,
    embedded,
    numer,
    denom,
    sums_out,
    sums_in,
    wide,
    mix_parts,
    back_out,
    back_in,
    part_out,
    part_in,
    table,
    row_sem,
    cell_sem,
    query_sem,
    sums_sem,
    halo_sem,
    chan_sem,
    table_sem,
):
    row_count = observed.shape[0]
    cap = rows_in.shape[1]
    nodes, width = node_embed.shape
    blocks = faces * slots
    face_nodes = slots * nodes
    face, slot, chan = lax.axis_index("face"), lax.axis_index("slot"), lax.axis_index("chan")
    block = face * slots + slot
    other = 1 - chan

    def block_id(index):
        return {"face": index // slots, "slot": lax.rem(index, slots)}

    barrier = pltpu.get_barrier_semaphore()

    def greet(k, carry):
        pl.semaphore_signal(
            barrier, inc=1, device_id=block_id(lax.rem(block + k, blocks)), device_id_type=MESH
        )
        return carry

    lax.fori_loop(1, blocks, greet, 0)
    pl.semaphore_signal(barrier, inc=1, device_id={"chan": other}, device_id_type=MESH)

    face_of = face_row[...]
    sub = lax.broadcasted_iota(jnp.int32, (max(8, faces), row_count), 0)
    lane = lax.broadcasted_iota(jnp.int32, (max(8, faces), row_count), 1)
    aimed = jnp.where(sub == face_of, 1, 0)
    count = aimed
    step = 1
    while step < row_count:
        count = count + jnp.where(lane >= step, pltpu.roll(count, step, 1), 0)
        step *= 2
    place = jnp.sum(aimed * (count - 1), axis=0, keepdims=True) + face_of * cap
    cell1 = cell_row[...] + 1
    sub16 = lax.broadcasted_iota(jnp.int32, (16, row_count), 0)
    cell_parts = (
        jnp.where(sub16 == 0, cell1 >> 7, jnp.where(sub16 == 1, cell1 & 127, 0))
        .astype(F32)
        .astype(BF16)
    )

    def bucket(goal):
        pick = ones_where(
            lax.broadcasted_iota(jnp.int32, (cap, row_count), 0) == place - goal * cap
        )
        parts = dot_nt(cell_parts, pick)
        cells = (parts[0:1] * 128.0 + parts[1:2]).astype(jnp.int32) - 1
        return dot(pick, observed[...]).astype(BF16), jnp.broadcast_to(cells, (8, cap))

    rows, cells = bucket(face)
    rows_in[0] = rows
    cells_in[0] = cells
    queries[pl.ds(slot * nodes, nodes)] = node_embed[...]

    pl.semaphore_wait(barrier, blocks)

    def query_copy(k):
        mine = queries.at[pl.ds(slot * nodes, nodes)]
        return pltpu.make_async_remote_copy(
            src_ref=node_embed,
            dst_ref=mine,
            send_sem=query_sem.at[0, k],
            recv_sem=query_sem.at[1, k],
            device_id={"slot": lax.rem(slot + k, slots)},
            device_id_type=MESH,
        )

    for k in range(1, slots):
        query_copy(k).start()

    def row_copy(k):
        return pltpu.make_async_remote_copy(
            src_ref=rows_out.at[k],
            dst_ref=rows_in.at[k],
            send_sem=row_sem.at[0, k],
            recv_sem=row_sem.at[1, k],
            device_id={"face": lax.rem(face + k, faces)},
            device_id_type=MESH,
        )

    def cell_copy(k):
        return pltpu.make_async_remote_copy(
            src_ref=cells_out.at[k],
            dst_ref=cells_in.at[k],
            send_sem=cell_sem.at[0, k],
            recv_sem=cell_sem.at[1, k],
            device_id={"face": lax.rem(face + k, faces)},
            device_id_type=MESH,
        )

    def send_rows(k, carry):
        rows, cells = bucket(lax.rem(face + k, faces))
        rows_out[k] = rows
        cells_out[k] = cells
        row_copy(k).start()
        cell_copy(k).start()
        return carry

    lax.fori_loop(1, faces, send_rows, 0)

    group = ones_where(
        lax.broadcasted_iota(jnp.int32, (width, LANES), 0) // HD
        == lax.broadcasted_iota(jnp.int32, (width, LANES), 1)
    )
    spread = ones_where(
        lax.broadcasted_iota(jnp.int32, (LANES, width), 1) // HD
        == lax.broadcasted_iota(jnp.int32, (LANES, width), 0)
    )
    numer[...] = jnp.zeros_like(numer)
    denom[...] = jnp.zeros_like(denom)

    for k in range(1, slots):
        query_copy(k).wait()

    def attend_block(k, carry):
        @pl.when(k > 0)
        def _():
            row_copy(k).wait()
            cell_copy(k).wait()

        x = rows_in[k]
        chunk = 256
        for j in range(0, w_embed.shape[1], chunk):
            embedded[:, j : j + chunk] = jax.nn.gelu(dot(x, w_embed[:, j : j + chunk])).astype(BF16)
        keys = dot(embedded[...], w_key[...]).astype(BF16).astype(F32)
        hit = ones_where(
            lax.broadcasted_iota(jnp.int32, (face_nodes, cap), 0) == cells_in[k][0:1]
        )
        picked = dot_tn(hit, queries[...])
        score = dot((picked * keys).astype(BF16), group) * (HD**-0.5)
        attend = jax.nn.sigmoid(score).astype(BF16)
        values = embedded[:, pl.ds(pl.multiple_of(chan * width, width), width)]
        contrib = (dot(attend, spread) * values.astype(F32)).astype(BF16)
        numer[...] += dot(hit, contrib)
        denom[...] += dot(hit, attend)
        return carry

    lax.fori_loop(0, faces, attend_block, 0)

    def sums_copy(k):
        return pltpu.make_async_remote_copy(
            src_ref=sums_out.at[k],
            dst_ref=sums_in.at[k],
            send_sem=sums_sem.at[0, k],
            recv_sem=sums_sem.at[1, k],
            device_id={"slot": lax.rem(slot + k, slots)},
            device_id_type=MESH,
        )

    for k in range(1, slots):
        theirs = pl.ds(lax.rem(slot + k, slots) * nodes, nodes)
        sums_out[k, :, :width] = numer[theirs].astype(BF16)
        sums_out[k, :, width:] = denom[theirs].astype(BF16)
        sums_copy(k).start()

    extended = nodes + 2 * HALO
    position = lax.broadcasted_iota(jnp.int32, (extended, nodes), 0)
    weights = jnp.zeros((extended, nodes), F32)
    for j in range(neighbours.shape[0]):
        weights += jnp.where(position == neighbours[j : j + 1], edge_weight[j : j + 1], 0.0)
    weights_high, weights_low = two_parts(weights)

    mine = pl.ds(slot * nodes, nodes)
    total = numer[mine]
    weight = denom[mine]
    for k in range(1, slots):
        sums_copy(k).wait()
        total += sums_in[k, :, :width].astype(F32)
        weight += sums_in[k, :, width:].astype(F32)
    weight_high, weight_low = two_parts(weight)
    weight = dot(weight_high, spread) + dot(weight_low, spread)
    latent = (node_embed[...].astype(F32) + total / (1.0 + weight)).astype(BF16)
    wide[HALO : HALO + nodes] = latent

    right = pltpu.make_async_remote_copy(
        src_ref=wide.at[pl.ds(nodes, HALO)],
        dst_ref=wide.at[pl.ds(0, HALO)],
        send_sem=halo_sem.at[0, 0],
        recv_sem=halo_sem.at[1, 0],
        device_id=block_id(lax.rem(block + 1, blocks)),
        device_id_type=MESH,
    )
    left = pltpu.make_async_remote_copy(
        src_ref=wide.at[pl.ds(HALO, HALO)],
        dst_ref=wide.at[pl.ds(HALO + nodes, HALO)],
        send_sem=halo_sem.at[0, 1],
        recv_sem=halo_sem.at[1, 1],
        device_id=block_id(lax.rem(block + blocks - 1, blocks)),
        device_id_type=MESH,
    )
    right.start()
    left.start()
    right.wait()
    left.wait()

    def chan_copy(k, source, goal):
        return pltpu.make_async_remote_copy(
            src_ref=source,
            dst_ref=goal,
            send_sem=chan_sem.at[0, k],
            recv_sem=chan_sem.at[1, k],
            device_id={"chan": other},
            device_id_type=MESH,
        )

    around = wide[...]
    summed = (dot_tn(weights_high, around) + dot_tn(weights_low, around)).astype(BF16)
    mix_parts[0] = summed
    mix_copy = chan_copy(0, mix_parts.at[0], mix_parts.at[1])
    mix_copy.start()
    mixed = dot(summed, w_mix[pl.ds(pl.multiple_of(chan * width, width), width)])
    mix_copy.wait()
    mixed += dot(mix_parts[1], w_mix[pl.ds(pl.multiple_of(other * width, width), width)])
    hidden = jax.nn.gelu(mixed).astype(BF16)
    back_out[...] = dot(
        hidden, w_back[:, pl.ds(pl.multiple_of(other * width, width), width)]
    ).astype(BF16)
    back_copy = chan_copy(1, back_out, back_in)
    back_copy.start()
    update = dot(hidden, w_back[:, pl.ds(pl.multiple_of(chan * width, width), width)])
    back_copy.wait()
    state = (latent.astype(F32) + update + back_in[...].astype(F32)).astype(BF16)
    state_out[...] = state

    part = dot(state, w_out[...])
    part_out[...] = part
    part_copy = chan_copy(2, part_out, part_in)
    part_copy.start()
    part_copy.wait()
    here = pl.ds(block * nodes, nodes)
    table[here] = (part + part_in[...]).astype(BF16)

    def table_copy(k):
        return pltpu.make_async_remote_copy(
            src_ref=table.at[here],
            dst_ref=table.at[here],
            send_sem=table_sem.at[0, k],
            recv_sem=table_sem.at[1, k],
            device_id=block_id(lax.rem(block + k, blocks)),
            device_id_type=MESH,
        )

    def send_table(k, carry):
        table_copy(k).start()
        return carry

    lax.fori_loop(1, blocks, send_table, 0)
    node_of = node_col[...]

    def decode(k, total):
        source = lax.rem(block + blocks - k, blocks)

        @pl.when(k > 0)
        def _():
            table_copy(k).wait()

        hit = ones_where(
            lax.broadcasted_iota(jnp.int32, (row_count, nodes), 1) == node_of - source * nodes
        )
        return total + dot(hit, table[pl.ds(source * nodes, nodes)])

    total = lax.fori_loop(0, blocks, decode, jnp.zeros(predicted.shape, F32))
    predicted[...] = total.astype(BF16)


def body(
    observed,
    target_face,
    target_cell,
    node_embed,
    neighbours,
    edge_weight,
    w_embed,
    w_key,
    w_mix,
    w_back,
    w_out,
):
    faces, slots = lax.axis_size("face"), lax.axis_size("slot")
    row_count, features = observed.shape
    nodes, width = node_embed.shape
    channels = w_embed.shape[1]
    cap = 2 * row_count // faces
    blocks = faces * slots
    face_row = target_face.reshape(1, row_count)
    cell_row = target_cell.reshape(1, row_count)
    node_col = target_face * (nodes * slots) + target_cell[:, None]
    vmem = pl.BlockSpec(memory_space=pltpu.VMEM)
    dma = pltpu.SemaphoreType.DMA
    return pl.pallas_call(
        functools.partial(kernel, faces, slots),
        out_shape=(
            jax.ShapeDtypeStruct((row_count, w_out.shape[1]), BF16),
            jax.ShapeDtypeStruct((nodes, width), BF16),
        ),
        in_specs=[vmem] * 12,
        out_specs=(vmem, vmem),
        scratch_shapes=[
            pltpu.VMEM((faces, cap, features), BF16),
            pltpu.VMEM((faces, cap, features), BF16),
            pltpu.VMEM((faces, 8, cap), jnp.int32),
            pltpu.VMEM((faces, 8, cap), jnp.int32),
            pltpu.VMEM((slots * nodes, width), BF16),
            pltpu.VMEM((cap, channels), BF16),
            pltpu.VMEM((slots * nodes, width), F32),
            pltpu.VMEM((slots * nodes, LANES), F32),
            pltpu.VMEM((slots, nodes, width + LANES), BF16),
            pltpu.VMEM((slots, nodes, width + LANES), BF16),
            pltpu.VMEM((nodes + 2 * HALO, width), BF16),
            pltpu.VMEM((2, nodes, width), BF16),
            pltpu.VMEM((nodes, width), BF16),
            pltpu.VMEM((nodes, width), BF16),
            pltpu.VMEM((nodes, w_out.shape[1]), F32),
            pltpu.VMEM((nodes, w_out.shape[1]), F32),
            pltpu.VMEM((blocks * nodes, w_out.shape[1]), BF16),
            dma((2, faces)),
            dma((2, faces)),
            dma((2, slots)),
            dma((2, slots)),
            dma((2, 2)),
            dma((2, 3)),
            dma((2, blocks)),
        ],
        compiler_params=pltpu.CompilerParams(
            collective_id=0, has_side_effects=True, vmem_limit_bytes=48 * 1024 * 1024
        ),
    )(
        observed,
        face_row,
        cell_row,
        node_col,
        node_embed,
        neighbours,
        edge_weight,
        w_embed,
        w_key,
        w_mix,
        w_back,
        w_out,
    )


def solution(mesh):
    in_specs = (
        P(("member", "face", "slot"), None),
        P(("member", "face", "slot"), None),
        P(("member", "face", "slot")),
        P(("face", "slot"), "chan"),
        P(None, ("face", "slot")),
        P(None, ("face", "slot")),
        P(),
        P(None, "chan"),
        P(None, "chan"),
        P("chan", None),
        P("chan", None),
    )
    out_specs = (P(("member", "face", "slot"), None), P(("member", "face", "slot"), "chan"))
    return jax.shard_map(body, mesh=mesh, in_specs=in_specs, out_specs=out_specs, check_vma=False)
```

time: 278 us -> 59.9 us (0.22)
  waiting for transfers between devices: 121 us -> 0 us
  local copies, waits for them, and re-layouts: 70.2 us -> 9.24 us
  Pallas kernels: 0 us -> 48.9 us
  starting transfers between devices: 24.8 us -> 0 us
  matrix products: 18 us -> 0 us
  blocking collectives: 15.5 us -> 0 us
  between operations: 14 us -> 0.69 us
  other arithmetic: 13.4 us -> 0.71 us
    all_to_all x4 -> x0, waiting for transfers between devices: 74.4 us -> none  [the longest x1 40.5 us: body(): lax.all_to_all(key_buffer, 'face', split_axis=0, concat_axis=0, tiled=True)]
    pallas_call x0 -> x1, Pallas kernels: none -> 48.9 us  [body(): pl.pallas_call(functools.partial(kernel, faces, slots), out_shape=(jax.Sh...]
    gather x4 -> x0, local copies, waits for them, and re-layouts: 25.1 us -> none  [the longest x1 9.18 us: body(): picked = queries[safe_cell]]
    reduce_scatter x2 -> x0, waiting for transfers between devices: 22.5 us -> none  [the longest x1 13.3 us: body(): lax.psum_scatter(numer.astype(jnp.bfloat16), 'slot', scatter_dimension=0,...]
    psum x1 -> x0, waiting for transfers between devices: 20.1 us -> none  [body(): answers = lax.psum(row_terms.astype(jnp.bfloat16), 'chan')]
    all_to_all x4 -> x0, starting transfers between devices: 19.9 us -> none  [the longest x1 6.32 us: body(): lax.all_to_all(cell_buffer, 'face', split_axis=0, concat_axis=0, tiled=True)]
    scatter x3 -> x0, local copies, waits for them, and re-layouts: 18.5 us -> none  [the longest x2 13.4 us: body(): jnp.zeros((faces * capacity, local_width), jnp.bfloat16).at[slot_index]]
    dot_general x6 -> x0, matrix products: 18 us -> none  [the longest x1 6.63 us: body(): jnp.einsum('rn,rc->nc', onehot, contrib, precision=lax.Precision.HIGHEST,...]
  transfers between devices with their start and end apart: 10 -> 0, of which waited for: 8 -> 0; matrix products, arithmetic and copies ran while one was open for 18% -> 0% of each run, Pallas kernels for 0% -> 0%
where the time goes in v1:
time: 59.9 us; the launch traced here: 59.5 us
  Pallas kernels  48.9 us (82%)
  local copies, waits for them, and re-layouts  9.24 us (15%)
  other arithmetic  0.71 us (1%)
  between operations  0.69 us (1%)
    pallas_call x1, Pallas kernels, body(): pl.pallas_call(functools.partial(kernel, faces, slots), out_shape=(jax.Sh...  48.9 us
    unnamed x24, local copies, waits for them, and re-layouts  9.02 us

profile of v1, /device:TPU:0, one launch (start us, length us, event | category | flops | bytes accessed | tf_op | source)
XLA Modules:
  0.0 59.5 jit_solution(7964482992075363100)
XLA Ops:
  0.6 0.0 copy-start.7
  0.6 0.7 %copy-done.7 = s32[1024,1]{0,1:T(1,128)S(1)} copy-done((s32[1024,1]{0,1:T(1,128)S(1)}, s32[1024,1]{0,1:T(1,128)}, u32[]{:S(2)}) %copy-start.7) | copy-done | bytes 4120
  1.3 0.0 copy-start.9
  1.3 0.7 %multiply_add_fusion = s32[1024,1]{0,1:T(1,128)S(1)} fusion(s32[1024,1]{0,1:T(1,128)} %bitcast.4, s32[1024,1]{0,1:T(1,128)S(1)} %copy-done.7), kind=kLoop, calls=%fused_computation | loop fusion | flops 2048 | bytes 12288 | tf_op jit(solution)/shard_map/add | solution.py:367
  2.0 0.0 copy-start.3
  2.0 0.0 copy-start.4
  2.0 0.0 copy-start.8
  2.0 0.2 copy.18.node_col
  2.3 0.0 copy-done.9
  2.3 0.7 %copy-done.3 = bf16[1024,128]{1,0:T(8,128)(2,1)S(1)} copy-done((bf16[1024,128]{1,0:T(8,128)(2,1)S(1)}, bf16[1024,128]{1,0:T(8,128)(2,1)}, u32[]{:S(2)}) %copy-start.3) | copy-done | bytes 262168
  3.0 0.1 copy-done.4
  3.1 0.0 copy-done.8
  3.1 0.0 copy-start
  3.1 1.2 %copy-done = bf16[1024,512]{1,0:T(8,128)(2,1)S(1)} copy-done((bf16[1024,512]{1,0:T(8,128)(2,1)S(1)}, bf16[1024,512]{1,0:T(8,128)(2,1)}, u32[]{:S(2)}) %copy-start) | copy-done | bytes 1048600
  4.3 0.0 copy-start.1
  4.3 1.2 %copy-done.1 = bf16[1024,512]{1,0:T(8,128)(2,1)S(1)} copy-done((bf16[1024,512]{1,0:T(8,128)(2,1)S(1)}, bf16[1024,512]{1,0:T(8,128)(2,1)}, u32[]{:S(2)}) %copy-start.1) | copy-done | bytes 1048600
  5.5 0.0 copy-start.2
  5.5 1.2 %copy-done.2 = bf16[512,1024]{1,0:T(8,128)(2,1)S(1)} copy-done((bf16[512,1024]{1,0:T(8,128)(2,1)S(1)}, bf16[512,1024]{1,0:T(8,128)(2,1)}, u32[]{:S(2)}) %copy-start.2) | copy-done | bytes 1048600
  6.7 0.0 copy-start.5
  6.7 0.9 %copy-done.5 = bf16[160,512]{1,0:T(8,128)(2,1)S(1)} copy-done((bf16[160,512]{1,0:T(8,128)(2,1)S(1)}, bf16[160,512]{1,0:T(8,128)(2,1)}, u32[]{:S(2)}) %copy-start.5) | copy-done | bytes 163864
  7.7 0.0 copy-start.6
  7.7 0.9 %copy-done.6 = bf16[512,128]{1,0:T(8,128)(2,1)S(1)} copy-done((bf16[512,128]{1,0:T(8,128)(2,1)S(1)}, bf16[512,128]{1,0:T(8,128)(2,1)}, u32[]{:S(2)}) %copy-start.6) | copy-done | bytes 131096
  8.6 0.0 copy-start.10
  8.6 0.7 %copy-done.10 = f32[6,160]{1,0:T(8,128)S(1)} copy-done((f32[6,160]{1,0:T(8,128)S(1)}, f32[6,160]{1,0:T(8,128)}, u32[]{:S(2)}) %copy-start.10) | copy-done | bytes 3864
  9.3 48.9 %shard_map.122 = (bf16[1024,128]{1,0:T(8,128)(2,1)S(1)}, bf16[160,512]{1,0:T(8,128)(2,1)S(1)}) custom-call(bf16[1024,128]{1,0:T(8,128)(2,1)S(1)} %copy-done.3, s32[1,1024]{1,0:T(1,128)S(1)} %bitcast.3, s32[1,1024]{1,0:T(1,128)S(1)} %bitcast.5, s32[1024,1]{1,0:T(8,128)S(1)} %copy.18.node_col, bf16[160,512]{1,0:T(8,128)(2,1)S(1)} %copy-done.5, ...), custom_call_target="tpu_custom_call" | custom-call | tf_op jit(solution)/shard_map/pallas_call | solution.py:370
  58.2 0.7 %copy.21 = bf16[1024,128]{1,0:T(8,128)(2,1)} copy(bf16[1024,128]{1,0:T(8,128)(2,1)S(1)} %get-tuple-element.4) | data formatting | bytes 524288
  58.9 0.7 %copy.22 = bf16[160,512]{1,0:T(8,128)(2,1)} copy(bf16[160,512]{1,0:T(8,128)(2,1)S(1)} %get-tuple-element.5) | data formatting | bytes 327680
Async XLA Ops:
  0.6 0.7 %copy-start.7 = (s32[1024,1]{0,1:T(1,128)S(1)}, s32[1024,1]{0,1:T(1,128)}, u32[]{:S(2)}) copy-start(s32[1024,1]{0,1:T(1,128)} %param.12) | copy-start | bytes 12292
  1.3 1.0 %copy-start.9 = (s32[6,160]{1,0:T(8,128)S(1)}, s32[6,160]{1,0:T(8,128)}, u32[]{:S(2)}) copy-start(s32[6,160]{1,0:T(8,128)} %neighbours.1) | copy-start | bytes 11524
  2.0 0.9 %copy-start.3 = (bf16[1024,128]{1,0:T(8,128)(2,1)S(1)}, bf16[1024,128]{1,0:T(8,128)(2,1)}, u32[]{:S(2)}) copy-start(bf16[1024,128]{1,0:T(8,128)(2,1)} %observed.1) | copy-start | bytes 786436
  2.0 1.0 %copy-start.4 = (bf16[128,1024]{1,0:T(8,128)(2,1)S(1)}, bf16[128,1024]{1,0:T(8,128)(2,1)}, u32[]{:S(2)}) copy-start(bf16[128,1024]{1,0:T(8,128)(2,1)} %w_embed.1) | copy-start | bytes 786436
  2.0 1.0 %copy-start.8 = (s32[1024]{0:T(1024)S(1)}, s32[1024]{0:T(1024)}, u32[]{:S(2)}) copy-start(s32[1024]{0:T(1024)} %param.13) | copy-start | bytes 12292
  3.1 1.2 %copy-start = (bf16[1024,512]{1,0:T(8,128)(2,1)S(1)}, bf16[1024,512]{1,0:T(8,128)(2,1)}, u32[]{:S(2)}) copy-start(bf16[1024,512]{1,0:T(8,128)(2,1)} %w_key.1) | copy-start | bytes 3145732
  4.3 1.2 %copy-start.1 = (bf16[1024,512]{1,0:T(8,128)(2,1)S(1)}, bf16[1024,512]{1,0:T(8,128)(2,1)}, u32[]{:S(2)}) copy-start(bf16[1024,512]{1,0:T(8,128)(2,1)} %w_mix.1) | copy-start | bytes 3145732
  5.5 1.2 %copy-start.2 = (bf16[512,1024]{1,0:T(8,128)(2,1)S(1)}, bf16[512,1024]{1,0:T(8,128)(2,1)}, u32[]{:S(2)}) copy-start(bf16[512,1024]{1,0:T(8,128)(2,1)} %w_back.1) | copy-start | bytes 3145732
  6.7 0.9 %copy-start.5 = (bf16[160,512]{1,0:T(8,128)(2,1)S(1)}, bf16[160,512]{1,0:T(8,128)(2,1)}, u32[]{:S(2)}) copy-start(bf16[160,512]{1,0:T(8,128)(2,1)} %node_embed.1) | copy-start | bytes 491524
  7.7 0.9 %copy-start.6 = (bf16[512,128]{1,0:T(8,128)(2,1)S(1)}, bf16[512,128]{1,0:T(8,128)(2,1)}, u32[]{:S(2)}) copy-start(bf16[512,128]{1,0:T(8,128)(2,1)} %w_out.1) | copy-start | bytes 393220
  8.6 0.7 %copy-start.10 = (f32[6,160]{1,0:T(8,128)S(1)}, f32[6,160]{1,0:T(8,128)}, u32[]{:S(2)}) copy-start(f32[6,160]{1,0:T(8,128)} %edge_weight.1) | copy-start | bytes 11524

commit v2 on v1

--- a/solution.py
+++ b/solution.py
@@ -10,6 +10,7 @@
 HD = 64
 HALO = 32
 LANES = 128
+INPUTS = 11
 MESH = pl.DeviceIdType.MESH
 F32 = jnp.float32
 BF16 = jnp.bfloat16
@@ -39,45 +40,58 @@
 def kernel(
     faces,
     slots,
-    observed,
-    face_row,
-    cell_row,
-    node_col,
-    node_embed,
-    neighbours,
-    edge_weight,
-    w_embed,
-    w_key,
-    w_mix,
-    w_back,
-    w_out,
-    predicted,
-    state_out,
-    rows_out,
-    rows_in,
-    cells_out,
-    cells_in,
-    queries,
-    embedded,
-    numer,
-    denom,
-    sums_out,
-    sums_in,
-    wide,
-    mix_parts,
-    back_out,
-    back_in,
-    part_out,
-    part_in,
-    table,
-    row_sem,
-    cell_sem,
-    query_sem,
-    sums_sem,
-    halo_sem,
-    chan_sem,
-    table_sem,
+    *refs,
 ):
+    arrays, refs = refs[:INPUTS], refs[INPUTS:]
+    predicted, state_out = refs[:2]
+    held, refs = refs[2 : 2 + INPUTS], refs[2 + INPUTS :]
+    (
+        load_sem,
+        rows_out,
+        rows_in,
+        cells_out,
+        cells_in,
+        queries,
+        embedded,
+        numer,
+        denom,
+        sums_out,
+        sums_in,
+        wide,
+        mix_parts,
+        back_out,
+        back_in,
+        part_out,
+        part_in,
+        table,
+        chosen,
+        row_sem,
+        cell_sem,
+        query_sem,
+        sums_sem,
+        halo_sem,
+        chan_sem,
+        table_sem,
+    ) = refs
+    loads = [
+        pltpu.make_async_copy(array, into, load_sem.at[i])
+        for i, (array, into) in enumerate(zip(arrays, held))
+    ]
+    for load in loads:
+        load.start()
+    (
+        face_row,
+        cell_row,
+        observed,
+        node_embed,
+        w_embed,
+        w_key,
+        neighbours,
+        edge_weight,
+        w_mix,
+        w_back,
+        w_out,
+    ) = held
     row_count = observed.shape[0]
     cap = rows_in.shape[1]
     nodes, width = node_embed.shape
@@ -100,6 +114,9 @@
 
     lax.fori_loop(1, blocks, greet, 0)
     pl.semaphore_signal(barrier, inc=1, device_id={"chan": other}, device_id_type=MESH)
+
+    for load in loads[:4]:
+        load.wait()
 
     face_of = face_row[...]
     sub = lax.broadcasted_iota(jnp.int32, (max(8, faces), row_count), 0)
@@ -189,6 +206,18 @@
     numer[...] = jnp.zeros_like(numer)
     denom[...] = jnp.zeros_like(denom)
 
+    node_of = jnp.broadcast_to(face_of * face_nodes + cell_row[...], (LANES, row_count)).T
+    lane_of = lax.broadcasted_iota(jnp.int32, (row_count, LANES), 1)
+    piece = chosen.shape[1]
+
+    def choose(first):
+        for j in range(0, piece, LANES):
+            chosen[:, j : j + LANES] = ones_where(lane_of == node_of - (first + j))
+
+    if piece == blocks * nodes:
+        choose(0)
+    for load in loads[4:6]:
+        load.wait()
     for k in range(1, slots):
         query_copy(k).wait()
 
@@ -232,6 +261,9 @@
         sums_out[k, :, :width] = numer[theirs].astype(BF16)
         sums_out[k, :, width:] = denom[theirs].astype(BF16)
         sums_copy(k).start()
+
+    for load in loads[6:]:
+        load.wait()
 
     extended = nodes + 2 * HALO
     position = lax.broadcasted_iota(jnp.int32, (extended, nodes), 0)
@@ -325,21 +357,22 @@
         return carry
 
     lax.fori_loop(1, blocks, send_table, 0)
-    node_of = node_col[...]
-
-    def decode(k, total):
-        source = lax.rem(block + blocks - k, blocks)
-
-        @pl.when(k > 0)
-        def _():
-            table_copy(k).wait()
-
-        hit = ones_where(
-            lax.broadcasted_iota(jnp.int32, (row_count, nodes), 1) == node_of - source * nodes
-        )
-        return total + dot(hit, table[pl.ds(source * nodes, nodes)])
-
-    total = lax.fori_loop(0, blocks, decode, jnp.zeros(predicted.shape, F32))
+
+    def take_table(k, carry):
+        table_copy(k).wait()
+        return carry
+
+    lax.fori_loop(1, blocks, take_table, 0)
+    if piece == blocks * nodes:
+        total = dot(chosen[...], table[...])
+    else:
+
+        def decode(k, total):
+            choose(k * piece)
+            return total + dot(chosen[...], table[pl.ds(k * piece, piece)])
+
+        total = jnp.zeros(predicted.shape, F32)
+        total = lax.fori_loop(0, blocks * nodes // piece, decode, total)
     predicted[...] = total.astype(BF16)
 
 
@@ -364,7 +397,20 @@
     blocks = faces * slots
     face_row = target_face.reshape(1, row_count)
     cell_row = target_cell.reshape(1, row_count)
-    node_col = target_face * (nodes * slots) + target_cell[:, None]
+    piece = blocks * nodes if blocks * nodes <= 4096 else slots * nodes
+    arrays = (
+        face_row,
+        cell_row,
+        observed,
+        node_embed,
+        w_embed,
+        w_key,
+        neighbours,
+        edge_weight,
+        w_mix,
+        w_back,
+        w_out,
+    )
     vmem = pl.BlockSpec(memory_space=pltpu.VMEM)
     dma = pltpu.SemaphoreType.DMA
     return pl.pallas_call(
@@ -373,9 +419,11 @@
             jax.ShapeDtypeStruct((row_count, w_out.shape[1]), BF16),
             jax.ShapeDtypeStruct((nodes, width), BF16),
         ),
-        in_specs=[vmem] * 12,
+        in_specs=[pl.BlockSpec(memory_space=pl.ANY)] * INPUTS,
         out_specs=(vmem, vmem),
-        scratch_shapes=[
+        scratch_shapes=[pltpu.VMEM(array.shape, array.dtype) for array in arrays]
+        + [
+            dma((INPUTS,)),
             pltpu.VMEM((faces, cap, features), BF16),
             pltpu.VMEM((faces, cap, features), BF16),
             pltpu.VMEM((faces, 8, cap), jnp.int32),
@@ -393,6 +441,7 @@
             pltpu.VMEM((nodes, w_out.shape[1]), F32),
             pltpu.VMEM((nodes, w_out.shape[1]), F32),
             pltpu.VMEM((blocks * nodes, w_out.shape[1]), BF16),
+            pltpu.VMEM((row_count, piece), BF16),
             dma((2, faces)),
             dma((2, faces)),
             dma((2, slots)),
@@ -402,22 +451,9 @@
             dma((2, blocks)),
         ],
         compiler_params=pltpu.CompilerParams(
-            collective_id=0, has_side_effects=True, vmem_limit_bytes=48 * 1024 * 1024
+            collective_id=0, has_side_effects=True, vmem_limit_bytes=60 * 1024 * 1024
         ),
-    )(
-        observed,
-        face_row,
-        cell_row,
-        node_col,
-        node_embed,
-        neighbours,
-        edge_weight,
-        w_embed,
-        w_key,
-        w_mix,
-        w_back,
-        w_out,
-    )
+    )(*arrays)
 
 
 def solution(mesh):

time: 59.9 us -> 52 us (0.87)
  local copies, waits for them, and re-layouts: 9.24 us -> 2.38 us
  other arithmetic: 0.71 us -> 0 us
    unnamed x24 -> x4, local copies, waits for them, and re-layouts: 9.02 us -> 2.38 us
    add x1 -> x0, other arithmetic: 0.71 us -> none  [body(): node_col = target_face * (nodes * slots) + target_cell[:, None]]
where the time goes in v2:
time: 52 us; the launch traced here: 51.8 us
  Pallas kernels  48.8 us (94%)
  local copies, waits for them, and re-layouts  2.38 us (5%)
  between operations  0.65 us (1%)
    pallas_call x1, Pallas kernels, body(): pl.pallas_call(functools.partial(kernel, faces, slots), out_shape=(jax.Sh...  48.8 us
    unnamed x4, local copies, waits for them, and re-layouts  2.38 us

profile of v2, /device:TPU:0, one launch (start us, length us, event | category | flops | bytes accessed | tf_op | source)
XLA Modules:
  0.0 51.8 jit_solution(1091230557939829576)
XLA Ops:
  0.6 48.8 %shard_map.122 = (bf16[1024,128]{1,0:T(8,128)(2,1)}, bf16[160,512]{1,0:T(8,128)(2,1)}) custom-call(s32[1,1024]{1,0:T(1,128)} %bitcast.2, s32[1,1024]{1,0:T(1,128)} %bitcast.3, bf16[1024,128]{1,0:T(8,128)(2,1)} %refs_2_.1, bf16[160,512]{1,0:T(8,128)(2,1)} %refs_3_.1, bf16[128,1024]{1,0:T(8,128)(2,1)} %refs_4_.1, bf16[1024,512]{1,0:T(8,128)(2,1)} %refs_5_.1, ...), custom_call_target="tpu_custom_call" | custom-call | tf_op jit(solution)/shard_map/pallas_call | solution.py:416
  49.4 0.0 copy-start
  49.4 1.7 %copy.15 = bf16[1024,128]{1,0:T(8,128)(2,1)} copy(bf16[1024,128]{1,0:T(8,128)(2,1)} %get-tuple-element.4) | data formatting | bytes 524288
  51.1 0.0 copy-done
  51.1 0.7 %copy.16 = bf16[160,512]{1,0:T(8,128)(2,1)} copy(bf16[160,512]{1,0:T(8,128)(2,1)S(1)} %copy-done) | data formatting | bytes 327680
Async XLA Ops:
  49.4 1.7 %copy-start = (bf16[160,512]{1,0:T(8,128)(2,1)S(1)}, bf16[160,512]{1,0:T(8,128)(2,1)}, u32[]{:S(2)}) copy-start(bf16[160,512]{1,0:T(8,128)(2,1)} %get-tuple-element.5) | copy-start | bytes 491524

commit v3 on v2

--- a/solution.py
+++ b/solution.py
@@ -57,6 +57,9 @@
         denom,
         sums_out,
         sums_in,
+        ends,
+        ends_out,
+        ends_in,
         wide,
         mix_parts,
         back_out,
@@ -66,12 +69,15 @@
         table,
         chosen,
         row_sem,
+        share_sem,
         cell_sem,
         query_sem,
         sums_sem,
         halo_sem,
+        ends_sem,
         chan_sem,
         table_sem,
+        core_sem,
     ) = refs
     loads = [
         pltpu.make_async_copy(array, into, load_sem.at[i])
@@ -142,11 +148,14 @@
         )
         parts = dot_nt(cell_parts, pick)
         cells = (parts[0:1] * 128.0 + parts[1:2]).astype(jnp.int32) - 1
-        return dot(pick, observed[...]).astype(BF16), jnp.broadcast_to(cells, (8, cap))
-
-    rows, cells = bucket(face)
-    rows_in[0] = rows
-    cells_in[0] = cells
+        return dot(pick, observed[...]).astype(BF16), cells
+
+    def fill(k, carry):
+        rows_out[k], cells_out[k] = bucket(lax.rem(face + k, faces))
+        return carry
+
+    rows_in[0], cells_in[0] = bucket(face)
+    lax.fori_loop(1, faces, fill, 0)
     queries[pl.ds(slot * nodes, nodes)] = node_embed[...]
 
     pl.semaphore_wait(barrier, blocks)
@@ -165,13 +174,27 @@
     for k in range(1, slots):
         query_copy(k).start()
 
+    share = cap // 2
+    own_share = pl.ds(chan * share, share)
+
     def row_copy(k):
         return pltpu.make_async_remote_copy(
-            src_ref=rows_out.at[k],
-            dst_ref=rows_in.at[k],
+            src_ref=rows_out.at[k, own_share],
+            dst_ref=rows_in.at[k, own_share],
             send_sem=row_sem.at[0, k],
             recv_sem=row_sem.at[1, k],
             device_id={"face": lax.rem(face + k, faces)},
+            device_id_type=MESH,
+        )
+
+    def share_copy(k, core):
+        rows = rows_in.at[k, pl.ds(core * share, share)]
+        return pltpu.make_async_remote_copy(
+            src_ref=rows,
+            dst_ref=rows,
+            send_sem=share_sem.at[0, k],
+            recv_sem=share_sem.at[1, k],
+            device_id={"chan": other},
             device_id_type=MESH,
         )
 
@@ -186,14 +209,27 @@
         )
 
     def send_rows(k, carry):
-        rows, cells = bucket(lax.rem(face + k, faces))
-        rows_out[k] = rows
-        cells_out[k] = cells
         row_copy(k).start()
         cell_copy(k).start()
         return carry
 
     lax.fori_loop(1, faces, send_rows, 0)
+
+    def edge_copy(side, source, goal, sem):
+        step = blocks - 1 if side == 0 else 1
+        return pltpu.make_async_remote_copy(
+            src_ref=source,
+            dst_ref=goal,
+            send_sem=halo_sem.at[0, sem],
+            recv_sem=halo_sem.at[1, sem],
+            device_id=block_id(lax.rem(block + step, blocks)),
+            device_id_type=MESH,
+        )
+
+    to_left = edge_copy(0, node_embed.at[pl.ds(0, HALO)], ends.at[1], 0)
+    to_right = edge_copy(1, node_embed.at[pl.ds(nodes - HALO, HALO)], ends.at[0], 1)
+    to_left.start()
+    to_right.start()
 
     group = ones_where(
         lax.broadcasted_iota(jnp.int32, (width, LANES), 0) // HD
@@ -224,14 +260,20 @@
     def attend_block(k, carry):
         @pl.when(k > 0)
         def _():
-            row_copy(k).wait()
             cell_copy(k).wait()
+            share_copy(k, other).wait_recv()
 
         x = rows_in[k]
         chunk = 256
         for j in range(0, w_embed.shape[1], chunk):
             embedded[:, j : j + chunk] = jax.nn.gelu(dot(x, w_embed[:, j : j + chunk])).astype(BF16)
         keys = dot(embedded[...], w_key[...]).astype(BF16).astype(F32)
+
+        @pl.when(k + 1 < faces)
+        def _():
+            row_copy(k + 1).wait()
+            share_copy(k + 1, chan).start()
+
         hit = ones_where(
             lax.broadcasted_iota(jnp.int32, (face_nodes, cap), 0) == cells_in[k][0:1]
         )
@@ -246,6 +288,12 @@
 
     lax.fori_loop(0, faces, attend_block, 0)
 
+    def finish_share(k, carry):
+        share_copy(k, chan).wait_send()
+        return carry
+
+    lax.fori_loop(1, faces, finish_share, 0)
+
     def sums_copy(k):
         return pltpu.make_async_remote_copy(
             src_ref=sums_out.at[k],
@@ -255,6 +303,51 @@
             device_id={"slot": lax.rem(slot + k, slots)},
             device_id_type=MESH,
         )
+
+    def end_goal(side, k):
+        return lax.rem(face * slots + k + (1 if side == 0 else blocks - 1), blocks)
+
+    def end_source(side, k):
+        step = blocks - 1 if side == 0 else 1
+        return lax.rem(block + step, blocks) // slots * slots + k
+
+    def end_copy(side, k, source_slot):
+        return pltpu.make_async_remote_copy(
+            src_ref=ends_out.at[side, k],
+            dst_ref=ends_in.at[side, slot],
+            send_sem=ends_sem.at[0, side, k],
+            recv_sem=ends_sem.at[1, side, source_slot],
+            device_id=block_id(end_goal(side, k)),
+            device_id_type=MESH,
+        )
+
+    def end_arrival(side, k):
+        return pltpu.make_async_remote_copy(
+            src_ref=ends_out.at[side, k],
+            dst_ref=ends_in.at[side, k],
+            send_sem=ends_sem.at[0, side, k],
+            recv_sem=ends_sem.at[1, side, k],
+            device_id=block_id(end_goal(side, k)),
+            device_id_type=MESH,
+        )
+
+    for side in range(2):
+        for k in range(slots):
+            edge = pl.ds(k * nodes + (nodes - HALO if side == 0 else 0), HALO)
+            sums = numer[edge].astype(BF16)
+            counts = denom[edge].astype(BF16)
+            away = end_goal(side, k) != block
+
+            @pl.when(away)
+            def _():
+                ends_out[side, k, :, :width] = sums
+                ends_out[side, k, :, width:] = counts
+                end_copy(side, k, slot).start()
+
+            @pl.when(jnp.logical_not(away))
+            def _():
+                ends_in[side, slot, :, :width] = sums
+                ends_in[side, slot, :, width:] = counts
 
     for k in range(1, slots):
         theirs = pl.ds(lax.rem(slot + k, slots) * nodes, nodes)
@@ -279,31 +372,32 @@
         sums_copy(k).wait()
         total += sums_in[k, :, :width].astype(F32)
         weight += sums_in[k, :, width:].astype(F32)
-    weight_high, weight_low = two_parts(weight)
-    weight = dot(weight_high, spread) + dot(weight_low, spread)
-    latent = (node_embed[...].astype(F32) + total / (1.0 + weight)).astype(BF16)
+
+    def latent_of(features, total, weight):
+        high, low = two_parts(weight)
+        weight = dot(high, spread) + dot(low, spread)
+        return (features.astype(F32) + total / (1.0 + weight)).astype(BF16)
+
+    latent = latent_of(node_embed[...], total, weight)
     wide[HALO : HALO + nodes] = latent
-
-    right = pltpu.make_async_remote_copy(
-        src_ref=wide.at[pl.ds(nodes, HALO)],
-        dst_ref=wide.at[pl.ds(0, HALO)],
-        send_sem=halo_sem.at[0, 0],
-        recv_sem=halo_sem.at[1, 0],
-        device_id=block_id(lax.rem(block + 1, blocks)),
-        device_id_type=MESH,
-    )
-    left = pltpu.make_async_remote_copy(
-        src_ref=wide.at[pl.ds(HALO, HALO)],
-        dst_ref=wide.at[pl.ds(HALO + nodes, HALO)],
-        send_sem=halo_sem.at[0, 1],
-        recv_sem=halo_sem.at[1, 1],
-        device_id=block_id(lax.rem(block + blocks - 1, blocks)),
-        device_id_type=MESH,
-    )
-    right.start()
-    left.start()
-    right.wait()
-    left.wait()
+    to_left.wait()
+    to_right.wait()
+    for side in range(2):
+        for k in range(slots):
+
+            @pl.when(end_goal(side, k) != block)
+            def _():
+                end_copy(side, k, slot).wait_send()
+
+            @pl.when(end_source(side, k) != block)
+            def _():
+                end_arrival(side, k).wait_recv()
+
+        both = ends_in[side, 0].astype(F32)
+        for k in range(1, slots):
+            both += ends_in[side, k].astype(F32)
+        first = 0 if side == 0 else HALO + nodes
+        wide[first : first + HALO] = latent_of(ends[side], both[:, :width], both[:, width:])
 
     def chan_copy(k, source, goal):
         return pltpu.make_async_remote_copy(
@@ -336,33 +430,54 @@
 
     part = dot(state, w_out[...])
     part_out[...] = part
-    part_copy = chan_copy(2, part_out, part_in)
+    half = nodes // 2
+    part_copy = chan_copy(2, part_out.at[pl.ds(other * half, half)], part_in)
     part_copy.start()
     part_copy.wait()
-    here = pl.ds(block * nodes, nodes)
-    table[here] = (part + part_in[...]).astype(BF16)
-
-    def table_copy(k):
-        return pltpu.make_async_remote_copy(
-            src_ref=table.at[here],
-            dst_ref=table.at[here],
-            send_sem=table_sem.at[0, k],
-            recv_sem=table_sem.at[1, k],
-            device_id=block_id(lax.rem(block + k, blocks)),
-            device_id_type=MESH,
-        )
-
-    def send_table(k, carry):
-        table_copy(k).start()
-        return carry
-
-    lax.fori_loop(1, blocks, send_table, 0)
-
-    def take_table(k, carry):
-        table_copy(k).wait()
-        return carry
-
-    lax.fori_loop(1, blocks, take_table, 0)
+    part = part_out[pl.ds(chan * half, half)] + part_in[...]
+    table[pl.ds(block * nodes + chan * half, half)] = part.astype(BF16)
+
+    def half_copy(k, place, core, sems, goal):
+        source = lax.rem(block + blocks - place, blocks)
+        rows = table.at[pl.ds(source * nodes + core * half, half)]
+        return pltpu.make_async_remote_copy(
+            src_ref=rows,
+            dst_ref=rows,
+            send_sem=sems.at[0, k],
+            recv_sem=sems.at[1, k],
+            device_id=goal,
+            device_id_type=MESH,
+        )
+
+    def to_block(k, place):
+        goal = block_id(lax.rem(block + k, blocks))
+        return half_copy(k, place, chan, table_sem, goal)
+
+    def to_chan(k, core):
+        return half_copy(k, k, core, core_sem, {"chan": other})
+
+    def start_block(k, carry):
+        to_block(k, 0).start()
+        return carry
+
+    def forward(k, carry):
+        to_block(k, k).wait_recv()
+        to_chan(k, chan).start()
+        return carry
+
+    def finish(k, carry):
+        @pl.when(k > 0)
+        def _():
+            to_block(k, 0).wait_send()
+
+        to_chan(k, chan).wait_send()
+        to_chan(k, other).wait_recv()
+        return carry
+
+    lax.fori_loop(1, blocks, start_block, 0)
+    to_chan(0, chan).start()
+    lax.fori_loop(1, blocks, forward, 0)
+    lax.fori_loop(0, blocks, finish, 0)
     if piece == blocks * nodes:
         total = dot(chosen[...], table[...])
     else:
@@ -426,28 +541,34 @@
             dma((INPUTS,)),
             pltpu.VMEM((faces, cap, features), BF16),
             pltpu.VMEM((faces, cap, features), BF16),
-            pltpu.VMEM((faces, 8, cap), jnp.int32),
-            pltpu.VMEM((faces, 8, cap), jnp.int32),
+            pltpu.VMEM((faces, 1, cap), jnp.int32),
+            pltpu.VMEM((faces, 1, cap), jnp.int32),
             pltpu.VMEM((slots * nodes, width), BF16),
             pltpu.VMEM((cap, channels), BF16),
             pltpu.VMEM((slots * nodes, width), F32),
             pltpu.VMEM((slots * nodes, LANES), F32),
             pltpu.VMEM((slots, nodes, width + LANES), BF16),
             pltpu.VMEM((slots, nodes, width + LANES), BF16),
+            pltpu.VMEM((2, HALO, width), BF16),
+            pltpu.VMEM((2, slots, HALO, width + LANES), BF16),
+            pltpu.VMEM((2, slots, HALO, width + LANES), BF16),
             pltpu.VMEM((nodes + 2 * HALO, width), BF16),
             pltpu.VMEM((2, nodes, width), BF16),
             pltpu.VMEM((nodes, width), BF16),
             pltpu.VMEM((nodes, width), BF16),
             pltpu.VMEM((nodes, w_out.shape[1]), F32),
-            pltpu.VMEM((nodes, w_out.shape[1]), F32),
+            pltpu.VMEM((nodes // 2, w_out.shape[1]), F32),
             pltpu.VMEM((blocks * nodes, w_out.shape[1]), BF16),
             pltpu.VMEM((row_count, piece), BF16),
+            dma((2, faces)),
             dma((2, faces)),
             dma((2, faces)),
             dma((2, slots)),
             dma((2, slots)),
             dma((2, 2)),
+            dma((2, 2, slots)),
             dma((2, 3)),
+            dma((2, blocks)),
             dma((2, blocks)),
         ],
         compiler_params=pltpu.CompilerParams(

time: 52 us -> 48.5 us (0.933)
  Pallas kernels: 48.8 us -> 45.2 us
    pallas_call x1, Pallas kernels: 48.8 us -> 45.2 us  [body(): pl.pallas_call(functools.partial(kernel, faces, slots), out_shape=(jax.Sh...]
where the time goes in v3:
time: 48.5 us; the launch traced here: 48.3 us
  Pallas kernels  45.2 us (93%)
  local copies, waits for them, and re-layouts  2.38 us (5%)
  between operations  0.65 us (1%)
    pallas_call x1, Pallas kernels, body(): pl.pallas_call(functools.partial(kernel, faces, slots), out_shape=(jax.Sh...  45.2 us
    unnamed x4, local copies, waits for them, and re-layouts  2.38 us

profile of v3, /device:TPU:0, one launch (start us, length us, event | category | flops | bytes accessed | tf_op | source)
XLA Modules:
  0.0 48.3 jit_solution(16572241563830162297)
XLA Ops:
  0.6 45.2 %shard_map.122 = (bf16[1024,128]{1,0:T(8,128)(2,1)}, bf16[160,512]{1,0:T(8,128)(2,1)}) custom-call(s32[1,1024]{1,0:T(1,128)} %bitcast.2, s32[1,1024]{1,0:T(1,128)} %bitcast.3, bf16[1024,128]{1,0:T(8,128)(2,1)} %refs_2_.1, bf16[160,512]{1,0:T(8,128)(2,1)} %refs_3_.1, bf16[128,1024]{1,0:T(8,128)(2,1)} %refs_4_.1, bf16[1024,512]{1,0:T(8,128)(2,1)} %refs_5_.1, ...), custom_call_target="tpu_custom_call" | custom-call | tf_op jit(solution)/shard_map/pallas_call | solution.py:531
  45.9 0.0 copy-start
  45.9 1.7 %copy.15 = bf16[1024,128]{1,0:T(8,128)(2,1)} copy(bf16[1024,128]{1,0:T(8,128)(2,1)} %get-tuple-element.4) | data formatting | bytes 524288
  47.6 0.0 copy-done
  47.6 0.7 %copy.16 = bf16[160,512]{1,0:T(8,128)(2,1)} copy(bf16[160,512]{1,0:T(8,128)(2,1)S(1)} %copy-done) | data formatting | bytes 327680
Async XLA Ops:
  45.9 1.7 %copy-start = (bf16[160,512]{1,0:T(8,128)(2,1)S(1)}, bf16[160,512]{1,0:T(8,128)(2,1)}, u32[]{:S(2)}) copy-start(bf16[160,512]{1,0:T(8,128)(2,1)} %get-tuple-element.5) | copy-start | bytes 491524

commit v4 on v3

--- a/solution.py
+++ b/solution.py
@@ -250,8 +250,6 @@
         for j in range(0, piece, LANES):
             chosen[:, j : j + LANES] = ones_where(lane_of == node_of - (first + j))
 
-    if piece == blocks * nodes:
-        choose(0)
     for load in loads[4:6]:
         load.wait()
     for k in range(1, slots):
@@ -365,6 +363,8 @@
         weights += jnp.where(position == neighbours[j : j + 1], edge_weight[j : j + 1], 0.0)
     weights_high, weights_low = two_parts(weights)
 
+    if piece == blocks * nodes:
+        choose(0)
     mine = pl.ds(slot * nodes, nodes)
     total = numer[mine]
     weight = denom[mine]

time: 48.5 us -> 48.5 us (level)
  no operation moved by 1% of the time
where the time goes in v4:
time: 48.5 us; the launch traced here: 48.3 us
  Pallas kernels  45.2 us (93%)
  local copies, waits for them, and re-layouts  2.38 us (5%)
  between operations  0.65 us (1%)
    pallas_call x1, Pallas kernels, body(): pl.pallas_call(functools.partial(kernel, faces, slots), out_shape=(jax.Sh...  45.2 us
    unnamed x4, local copies, waits for them, and re-layouts  2.38 us

profile of v4, /device:TPU:0, one launch (start us, length us, event | category | flops | bytes accessed | tf_op | source)
XLA Modules:
  0.0 48.3 jit_solution(17650144322841903896)
XLA Ops:
  0.6 45.2 %shard_map.122 = (bf16[1024,128]{1,0:T(8,128)(2,1)}, bf16[160,512]{1,0:T(8,128)(2,1)}) custom-call(s32[1,1024]{1,0:T(1,128)} %bitcast.2, s32[1,1024]{1,0:T(1,128)} %bitcast.3, bf16[1024,128]{1,0:T(8,128)(2,1)} %refs_2_.1, bf16[160,512]{1,0:T(8,128)(2,1)} %refs_3_.1, bf16[128,1024]{1,0:T(8,128)(2,1)} %refs_4_.1, bf16[1024,512]{1,0:T(8,128)(2,1)} %refs_5_.1, ...), custom_call_target="tpu_custom_call" | custom-call | tf_op jit(solution)/shard_map/pallas_call | solution.py:531
  45.9 0.0 copy-start
  45.9 1.7 %copy.15 = bf16[1024,128]{1,0:T(8,128)(2,1)} copy(bf16[1024,128]{1,0:T(8,128)(2,1)} %get-tuple-element.4) | data formatting | bytes 524288
  47.6 0.0 copy-done
  47.6 0.7 %copy.16 = bf16[160,512]{1,0:T(8,128)(2,1)} copy(bf16[160,512]{1,0:T(8,128)(2,1)S(1)} %copy-done) | data formatting | bytes 327680
Async XLA Ops:
  45.9 1.7 %copy-start = (bf16[160,512]{1,0:T(8,128)(2,1)S(1)}, bf16[160,512]{1,0:T(8,128)(2,1)}, u32[]{:S(2)}) copy-start(bf16[160,512]{1,0:T(8,128)(2,1)} %get-tuple-element.5) | copy-start | bytes 491524
